TPU v7x, 32 devices: a whole 2x2x4 slice. The times are simulated.
32 devices in a mesh: section: 4 (over y, x), group: 8 (over z, core).
Axes of the slice: x: 2, y: 2, z: 4, core: 2. Of those that a mesh axis runs over, the one named last changes fastest.
Arguments:
- hidden: bfloat16 [512, 8, 1024], P('group', None, 'section'), may hold values from -6 to 6
- pre_weight: bfloat16 [7, 1024, 512], replicated, may hold values from -0.0625 to 0.0625
- up1_weight: bfloat16 [16, 512, 256], replicated, may hold values from -0.1875 to 0.1875
- up2_weight: bfloat16 [16, 256, 128], replicated, may hold values from -0.25 to 0.25
- up3_weight: bfloat16 [4, 128, 64], replicated, may hold values from -0.375 to 0.375
- res3_weight: bfloat16 [3, 64, 64], replicated, may hold values from -0.4375 to 0.4375
- up4_weight: bfloat16 [4, 64, 32], replicated, may hold values from -0.5 to 0.5
- res4_weight: bfloat16 [3, 32, 32], replicated, may hold values from -0.625 to 0.625
- post_weight: bfloat16 [7, 32], replicated, may hold values from -0.375 to 0.375
- owner_device: int32 [512, 1], replicated, may hold values from 0 to 7; in each aligned block of 16 rows (0 to 15, 16 to 31, ...) at most 8 rows name the same one
- stream_slot: int32 [512], replicated, may hold values from 0 to 3
- start_frame: int32 [512], replicated, may hold values from 0 to 56
- lead_frames: int32 [512], replicated, may hold values from 1 to 4
- tail_frames: int32 [512], replicated, may hold values from 1 to 4
Outputs:
- waveform: float32 [32, 4, 16384], P('group', 'section')
Inputs may be any that keep to these rules, and one draw needn't show every extreme that they name: `owner_device`: in each aligned block of 16 groups (the groups of one device), no owner is named by more than 8 groups, a bound that some block reaches.
All inputs are finite; a program needn't handle non-finite values.
Results may differ from a plain program's by a relative error of at most 0.015.
Values may be sent and summed in bfloat16 or wider, within the bound.
A program may use at most 128 MiB of HBM per device.

v0:
```python
import functools

import jax
import jax.numpy as jnp
from jax import lax
from jax.experimental import pallas as pl
from jax.experimental.pallas import tpu as pltpu
from jax.sharding import PartitionSpec as P

HOP = 256
STR_DEV = 4
SLF = 64
PAIRS = 32
CHUNK = 4
MESH = pl.DeviceIdType.MESH
F32 = jnp.float32
BF16 = jnp.bfloat16


def leaky(values, slope):
    return jnp.maximum(values, slope * values)


def iota(shape, dim):
    return lax.broadcasted_iota(jnp.int32, shape, dim)


def dot(lhs, rhs):
    return jnp.dot(lhs, rhs, preferred_element_type=F32)


def dot_nt(lhs, rhs):
    return lax.dot_general(lhs, rhs, (((1,), (1,)), ((), ())), preferred_element_type=F32)


def shifted(values, step, frames):
    rows = values.shape[0]
    frame = iota(values.shape, 0) & (frames - 1)
    moved = pltpu.roll(values, (-step) % rows, 0)
    inside = (frame + step >= 0) & (frame + step < frames)
    return jnp.where(inside, moved, 0.0)


def assemble(out_ref, spread, times, columns, tap_of):
    depth, width = spread[0].shape
    per_column = width // len(columns)
    column = iota((depth, width), 1) // per_column
    for place, time in enumerate(times):
        block = jnp.zeros((depth, width), F32)
        for at, out_time in enumerate(columns):
            tap = tap_of(time, out_time)
            if tap is not None:
                block = jnp.where(column == at, spread[tap], block)
        out_ref[place * depth : (place + 1) * depth, :] = block.astype(BF16)


def spread_taps(w_ref, copies):
    taps, _, width = w_ref.shape
    lanes = width * copies
    repeat = ((iota((width, lanes), 1) & (width - 1)) == iota((width, lanes), 0)).astype(F32).astype(BF16)
    return [dot(w_ref[tap], repeat) for tap in range(taps)]


def up_tap(time, out_time):
    tap = out_time + 1 - 2 * time
    return tap if 0 <= tap < 4 else None


def res_tap(time, out_time):
    step = time - out_time
    return step // 3 + 1 if step in (-3, 0, 3) else None


def kernel(
    sections,
    lanes,
    hidden_ref,
    pre_hbm,
    up1_hbm,
    up2_hbm,
    up3_ref,
    res3_ref,
    up4_ref,
    res4_ref,
    post_ref,
    owner_ref,
    slot_ref,
    start_ref,
    lead_ref,
    tail_ref,
    out_ref,
    x_ref,
    pre_ref,
    up1_ref,
    up2_ref,
    a1_ref,
    a_ref,
    i_ref,
    u_ref,
    w3_ref,
    r3_ref,
    w4_ref,
    r4_ref,
    wp_ref,
    place_ref,
    wave_ref,
    weight_sem,
    own_sem,
    hid_send,
    hid_recv,
    wave_send,
    wave_recv,
    fwd_send,
    fwd_recv,
):
    section = lax.axis_index("section")
    lane = lax.axis_index("group")
    chips = lanes // 2
    chip, core = lane // 2, lane % 2
    sibling = chip * 2 + (1 - core)
    rows = x_ref.shape[0] // sections
    frames = 8
    groups = rows // frames

    def block(index):
        return pl.ds(pl.multiple_of(index * rows, rows), rows)

    copies = [
        pltpu.make_async_copy(pre_hbm, pre_ref, weight_sem.at[0]),
        pltpu.make_async_copy(up1_hbm, up1_ref, weight_sem.at[1]),
        pltpu.make_async_copy(up2_hbm, up2_ref, weight_sem.at[2]),
    ]
    own = pltpu.make_async_copy(hidden_ref.at[block(section)], x_ref.at[block(section)], own_sem)

    barrier = pltpu.get_barrier_semaphore()
    for step in range(1, sections):
        pl.semaphore_signal(
            barrier, inc=1, device_id={"section": (section + step) % sections}, device_id_type=MESH
        )
    for step in range(1, chips):
        pl.semaphore_signal(
            barrier, inc=1, device_id={"group": ((chip + step) % chips) * 2 + core}, device_id_type=MESH
        )
    pl.semaphore_signal(barrier, inc=1, device_id={"group": sibling}, device_id_type=MESH)
    own.start()
    for copy in copies:
        copy.start()
    pl.semaphore_wait(barrier, sections + chips - 1)

    hidden_copies = []
    for step in range(1, sections):
        peer = (section + step) % sections
        hidden_copies.append(
            pltpu.make_async_remote_copy(
                src_ref=hidden_ref.at[block(peer)],
                dst_ref=x_ref.at[block(section)],
                send_sem=hid_send.at[step],
                recv_sem=hid_recv.at[step],
                device_id={"section": peer},
                device_id_type=MESH,
            )
        )
        hidden_copies[-1].start()

    assemble(w3_ref, spread_taps(up3_ref, 4), range(-1, 3), range(4), up_tap)
    assemble(r3_ref, spread_taps(res3_ref, 4), range(-4, 8), range(4), res_tap)
    assemble(w4_ref, spread_taps(up4_ref, 8), range(-2, 6), range(8), up_tap)
    assemble(r4_ref, spread_taps(res4_ref, 8), range(-4, 12), range(8), res_tap)
    post = post_ref[...].astype(F32)
    channels = post.shape[1]
    span = CHUNK * HOP // PAIRS
    eye = (iota((channels, channels), 0) == iota((channels, channels), 1)).astype(F32).astype(BF16)
    post_taps = [
        dot_nt(eye, jnp.broadcast_to(post[tap : tap + 1], (128, channels)).astype(BF16)) for tap in range(7)
    ]
    out_time = iota((channels, 128), 1) & (span - 1)
    for place, time in enumerate(range(-4, span + 4)):
        entry = jnp.zeros((channels, 128), F32)
        for tap in range(7):
            entry = jnp.where(out_time == time - tap + 3, post_taps[tap], entry)
        wp_ref[place * channels : (place + 1) * channels, :] = entry.astype(BF16)

    total = owner_ref.shape[1]
    which = iota((16, total), 0)
    facts = jnp.where(
        which == 0,
        owner_ref[...],
        jnp.where(
            which == 1,
            slot_ref[...] * SLF + start_ref[...],
            jnp.where(which == 2, lead_ref[...], jnp.where(which == 3, tail_ref[...], 0)),
        ),
    )
    facts = facts.astype(F32).astype(BF16)
    lane_groups = sections * groups
    per_tile = 128 // lane_groups
    row_group = iota((rows, total), 0) // frames
    mine = (iota((rows, total), 1) == lane * lane_groups + section * groups + row_group).astype(F32).astype(BF16)
    fades = dot_nt(mine, facts)
    lead, tail = fades[:, 2:3], fades[:, 3:4]
    column_group = iota((128, rows), 1) // frames
    column_frame = iota((1, rows), 1) & (frames - 1)
    target_row = iota((STR_DEV * SLF, rows), 0)
    for sub in range(per_tile):
        pick = (iota((128, rows), 0) == sub * lane_groups + section * groups + column_group).astype(F32).astype(BF16)
        for tile in range(total // 128):
            source = tile * per_tile + sub
            found = dot(facts[:, tile * 128 : (tile + 1) * 128], pick)
            owner = found[0:1].astype(jnp.int32)
            target = jnp.where(owner == lane, found[1:2].astype(jnp.int32) + column_frame, -1)
            place_ref[:, source * rows : (source + 1) * rows] = (
                (target_row == target).astype(F32).astype(BF16)
            )

    own.wait()
    copies[0].wait()
    for copy in hidden_copies:
        copy.wait()
    x = jnp.concatenate([x_ref[part * rows : (part + 1) * rows, :] for part in range(sections)], axis=1)
    projected = dot(x, pre_ref[3])
    for tap in (0, 1, 2, 4, 5, 6):
        projected = projected + shifted(dot(x, pre_ref[tap]), tap - 3, frames)
    active = leaky(projected, 0.1)
    now = active.astype(BF16)
    before = shifted(active, -1, frames).astype(BF16)
    after = shifted(active, 1, frames).astype(BF16)

    copies[1].wait()
    for phase in range(8):
        other, tap = (before, phase + 12) if phase < 4 else (after, phase - 4)
        up = dot(now, up1_ref[phase + 4]) + dot(other, up1_ref[tap])
        a1_ref[(phase + 1) * rows : (phase + 2) * rows, :] = leaky(up, 0.1).astype(BF16)

    def fill_ends(ref, count):
        last = ref[count * rows : (count + 1) * rows, :].astype(F32)
        ref[0:rows, :] = shifted(last, -1, frames).astype(BF16)
        first = ref[rows : 2 * rows, :].astype(F32)
        ref[(count + 1) * rows : (count + 2) * rows, :] = shifted(first, 1, frames).astype(BF16)

    fill_ends(a1_ref, 8)

    copies[2].wait()
    for pair in range(4):
        near = 2 * pair + 4
        far, offset = (2 * pair + 12, 0) if pair < 2 else (2 * pair - 4, 2)
        near_w = jnp.concatenate([up2_ref[near], up2_ref[near + 1]], axis=1)
        far_w = jnp.concatenate([up2_ref[far], up2_ref[far + 1]], axis=1)
        for half in range(2):
            low = half * 4
            here = a1_ref[(low + 1) * rows : (low + 5) * rows, :]
            there = a1_ref[(low + offset) * rows : (low + offset + 4) * rows, :]
            up = leaky(dot(here, near_w) + dot(there, far_w), 0.1).astype(BF16)
            for phase in range(4):
                to = (low + phase) * 4 + pair + 1
                a_ref[to * rows : (to + 1) * rows, :] = up[phase * rows : (phase + 1) * rows]
    fill_ends(a_ref, PAIRS)

    size = CHUNK * rows

    def each_chunk(body):
        def step(chunk, carry):
            body(pl.multiple_of(chunk * size, size))
            return carry

        lax.fori_loop(0, PAIRS // CHUNK, step, 0)

    def around(ref, at, whole):
        low = ref[pl.ds(at, size), :]
        mid = ref[pl.ds(pl.multiple_of(at + rows, rows), size), :]
        high = ref[pl.ds(pl.multiple_of(at + 2 * rows, rows), size), :]
        if not whole:
            low, high = low[:, 128:], high[:, :128]
        return jnp.concatenate([low, mid, high], axis=1)

    def upsample(w_ref):
        def body(at):
            up = dot(around(a_ref, at, False), w_ref[...])
            u_ref[pl.ds(at, size), :] = up
            i_ref[pl.ds(pl.multiple_of(at + rows, rows), size), :] = leaky(up, 0.1).astype(BF16)

        each_chunk(body)
        fill_ends(i_ref, PAIRS)

    def residual(w_ref, whole, slope):
        def body(at):
            middle = u_ref[pl.ds(at, size), :] + dot(around(i_ref, at, whole), w_ref[...])
            a_ref[pl.ds(pl.multiple_of(at + rows, rows), size), :] = leaky(middle, slope).astype(BF16)

        each_chunk(body)
        fill_ends(a_ref, PAIRS)

    upsample(w3_ref)
    residual(r3_ref, True, 0.1)
    upsample(w4_ref)
    residual(r4_ref, False, 0.01)

    post_w = wp_ref[...]
    halves = []
    column = iota((rows, 128), 1) // span
    for half in range(2):
        merged = jnp.zeros((rows, 128), F32)
        for part in range(128 // span):
            first = (half * (128 // span) + part) * CHUNK
            pieces = [a_ref[first * rows : (first + 1) * rows, 128:]]
            pieces += [a_ref[(first + 1 + p) * rows : (first + 2 + p) * rows, :] for p in range(CHUNK)]
            pieces += [a_ref[(first + 1 + CHUNK) * rows : (first + 2 + CHUNK) * rows, :128]]
            merged = jnp.where(column == part, dot(jnp.concatenate(pieces, axis=1), post_w), merged)
        halves.append(merged)
    wave = jnp.tanh(jnp.concatenate(halves, axis=1))
    frame = iota((rows, HOP), 0) & (frames - 1)
    sample = (frame * HOP + iota((rows, HOP), 1)).astype(F32) + 0.5
    ramp_in = jnp.minimum(1.0, sample / (HOP * lead))
    ramp_out = jnp.minimum(1.0, (frames * HOP - sample) / (HOP * tail))
    wave_ref[block(lane), :] = (wave * (ramp_in * ramp_out)).astype(BF16)

    def send(index, peer, send_sem, recv_sem):
        return pltpu.make_async_remote_copy(
            src_ref=wave_ref.at[block(index)],
            dst_ref=wave_ref.at[block(index)],
            send_sem=send_sem,
            recv_sem=recv_sem,
            device_id={"group": peer},
            device_id_type=MESH,
        )

    direct = []
    for step in range(1, chips):
        direct.append(send(lane, ((chip + step) % chips) * 2 + core, wave_send.at[step], wave_recv.at[step]))
        direct[-1].start()
    to_sibling = [send(lane, sibling, fwd_send.at[0], fwd_recv.at[0])]
    to_sibling[0].start()
    for step in range(1, chips):
        direct[step - 1].wait_recv()
        source = ((chip - step + chips) % chips) * 2 + core
        to_sibling.append(send(source, sibling, fwd_send.at[step], fwd_recv.at[step]))
        to_sibling[-1].start()
    for copy in to_sibling:
        copy.wait_recv()
    placed = dot(place_ref[...], wave_ref[...])
    out_ref[pl.ds(0, STR_DEV * SLF, stride=2), :] = placed[:, :128]
    out_ref[pl.ds(1, STR_DEV * SLF, stride=2), :] = placed[:, 128:]
    for copy in direct + to_sibling:
        copy.wait_send()


def shards(
    hidden,
    pre_weight,
    up1_weight,
    up2_weight,
    up3_weight,
    res3_weight,
    up4_weight,
    res4_weight,
    post_weight,
    owner_device,
    stream_slot,
    start_frame,
    lead_frames,
    tail_frames,
):
    sections = lax.axis_size("section")
    lanes = lax.axis_size("group")
    per_device = hidden.shape[0] // sections
    frames, width = hidden.shape[1], hidden.shape[2]
    rows = per_device * frames
    chips = lanes // 2
    total = stream_slot.shape[0]
    vmem = pl.BlockSpec(memory_space=pltpu.VMEM)
    hbm = pl.BlockSpec(memory_space=pl.ANY)
    blocks = PAIRS + 2
    out = pl.pallas_call(
        functools.partial(kernel, sections, lanes),
        out_shape=jax.ShapeDtypeStruct((STR_DEV * SLF * HOP // 128, 128), F32),
        in_specs=[hbm] * 4 + [vmem] * 10,
        out_specs=vmem,
        scratch_shapes=[
            pltpu.VMEM((sections * rows, width), BF16),
            pltpu.VMEM(pre_weight.shape, BF16),
            pltpu.VMEM(up1_weight.shape, BF16),
            pltpu.VMEM(up2_weight.shape, BF16),
            pltpu.VMEM((10 * rows, 256), BF16),
            pltpu.VMEM((blocks * rows, 256), BF16),
            pltpu.VMEM((blocks * rows, 256), BF16),
            pltpu.VMEM((PAIRS * rows, 256), F32),
            pltpu.VMEM((512, 256), BF16),
            pltpu.VMEM((768, 256), BF16),
            pltpu.VMEM((512, 256), BF16),
            pltpu.VMEM((512, 256), BF16),
            pltpu.VMEM(((CHUNK * HOP // PAIRS + 8) * 32, 128), BF16),
            pltpu.VMEM((STR_DEV * SLF, lanes * rows), BF16),
            pltpu.VMEM((lanes * rows, HOP), BF16),
            pltpu.SemaphoreType.DMA((3,)),
            pltpu.SemaphoreType.DMA,
            pltpu.SemaphoreType.DMA((sections,)),
            pltpu.SemaphoreType.DMA((sections,)),
            pltpu.SemaphoreType.DMA((chips,)),
            pltpu.SemaphoreType.DMA((chips,)),
            pltpu.SemaphoreType.DMA((chips,)),
            pltpu.SemaphoreType.DMA((chips,)),
        ],
        compiler_params=pltpu.CompilerParams(
            collective_id=0, has_side_effects=True, vmem_limit_bytes=48 * 1024 * 1024
        ),
        name="vocoder",
    )(
        hidden.reshape(sections * rows, width),
        pre_weight,
        up1_weight,
        up2_weight,
        up3_weight,
        res3_weight,
        up4_weight,
        res4_weight,
        post_weight,
        owner_device.reshape(1, total),
        stream_slot.reshape(1, total),
        start_frame.reshape(1, total),
        lead_frames.reshape(1, total),
        tail_frames.reshape(1, total),
    )
    return out.reshape(STR_DEV, 1, SLF * HOP)


def solution(mesh):
    in_specs = (P("group", None, "section"),) + (P(),) * 13
    return jax.shard_map(
        shards, mesh=mesh, in_specs=in_specs, out_specs=P("group", "section", None), check_vma=False
    )
```

profile of v0, /device:TPU:5, one launch (start us, length us, event | category | flops | bytes accessed | tf_op | source)
XLA Modules:
  0.0 43.3 jit_solution(10351438922222292959)
XLA Ops:
  0.0 0.9 %copy.16.up4_ref = bf16[4,64,32]{2,1,0:T(8,128)(2,1)S(1)} copy(bf16[4,64,32]{1,2,0:T(8,128)(2,1)} %param.20) | data formatting | bytes 32768 | tf_op args[6]
  0.9 1.0 %copy.15.up3_ref = bf16[4,128,64]{2,1,0:T(8,128)(2,1)S(1)} copy(bf16[4,128,64]{1,2,0:T(8,128)(2,1)} %param.18) | data formatting | bytes 131072 | tf_op args[4]
  1.8 0.0 copy-start
  1.8 2.2 %copy-done = bf16[16,512,256]{2,1,0:T(8,128)(2,1)S(1)} copy-done((bf16[16,512,256]{2,1,0:T(8,128)(2,1)S(1)}, bf16[16,512,256]{2,1,0:T(8,128)(2,1)}, u32[]{:S(2)}) %copy-start) | copy-done | bytes 4194328
  4.0 0.0 copy-start.1
  4.0 1.2 %copy-done.1 = bf16[16,256,128]{2,1,0:T(8,128)(2,1)S(1)} copy-done((bf16[16,256,128]{2,1,0:T(8,128)(2,1)S(1)}, bf16[16,256,128]{2,1,0:T(8,128)(2,1)}, u32[]{:S(2)}) %copy-start.1) | copy-done | bytes 1048600
  5.2 0.0 copy-start.2
  5.2 0.9 %copy-done.2 = bf16[64,8,256]{2,1,0:T(8,128)(2,1)S(1)} copy-done((bf16[64,8,256]{2,1,0:T(8,128)(2,1)S(1)}, bf16[64,8,256]{2,1,0:T(8,128)(2,1)}, u32[]{:S(2)}) %copy-start.2) | copy-done | bytes 262168
  6.2 0.0 copy-start.3
  6.2 0.8 %copy-done.3 = bf16[3,64,64]{2,1,0:T(8,128)(2,1)S(1)} copy-done((bf16[3,64,64]{2,1,0:T(8,128)(2,1)S(1)}, bf16[3,64,64]{2,1,0:T(8,128)(2,1)}, u32[]{:S(2)}) %copy-start.3) | copy-done | bytes 24600
  7.0 0.0 copy-start.4
  7.0 0.7 %copy-done.4 = bf16[3,32,32]{2,1,0:T(8,128)(2,1)S(1)} copy-done((bf16[3,32,32]{2,1,0:T(8,128)(2,1)S(1)}, bf16[3,32,32]{2,1,0:T(8,128)(2,1)}, u32[]{:S(2)}) %copy-start.4) | copy-done | bytes 6168
  7.7 0.0 copy-start.5
  7.7 0.7 %copy-done.5 = bf16[7,32]{1,0:T(8,128)(2,1)S(1)} copy-done((bf16[7,32]{1,0:T(8,128)(2,1)S(1)}, bf16[7,32]{1,0:T(8,128)(2,1)}, u32[]{:S(2)}) %copy-start.5) | copy-done | bytes 472
  8.4 0.0 copy-start.6
  8.4 0.7 %copy-done.6 = s32[512,1]{0,1:T(1,128)S(1)} copy-done((s32[512,1]{0,1:T(1,128)S(1)}, s32[512,1]{0,1:T(1,128)}, u32[]{:S(2)}) %copy-start.6) | copy-done | bytes 2072
  9.1 0.0 copy-start.7
  9.1 0.7 %copy-done.7 = s32[512]{0:T(512)S(1)} copy-done((s32[512]{0:T(512)S(1)}, s32[512]{0:T(512)}, u32[]{:S(2)}) %copy-start.7) | copy-done | bytes 2072
  9.8 0.0 copy-start.8
  9.8 0.7 %copy-done.8 = s32[512]{0:T(512)S(1)} copy-done((s32[512]{0:T(512)S(1)}, s32[512]{0:T(512)}, u32[]{:S(2)}) %copy-start.8) | copy-done | bytes 2072
  10.5 0.0 copy-start.9
  10.5 0.7 %copy-done.9 = s32[512]{0:T(512)S(1)} copy-done((s32[512]{0:T(512)S(1)}, s32[512]{0:T(512)}, u32[]{:S(2)}) %copy-start.9) | copy-done | bytes 2072
  11.1 0.0 copy-start.10
  11.1 0.7 %copy-done.10 = s32[512]{0:T(512)S(1)} copy-done((s32[512]{0:T(512)S(1)}, s32[512]{0:T(512)}, u32[]{:S(2)}) %copy-start.10) | copy-done | bytes 2072
  11.8 30.7 %vocoder.1 = f32[512,128]{1,0:T(8,128)S(1)} custom-call(bf16[512,256]{1,0:T(8,128)(2,1)S(1)} %bitcast.8, bf16[7,1024,512]{2,1,0:T(8,128)(2,1)} %pre_hbm.1, bf16[16,512,256]{2,1,0:T(8,128)(2,1)S(1)} %copy-done, bf16[16,256,128]{2,1,0:T(8,128)(2,1)S(1)} %copy-done.1, bf16[4,128,64]{2,1,0:T(8,128)(2,1)S(1)} %copy.15.up3_ref, bf16[3,64,64]{2,1,0:T(8,128)(2,1)S(1)} %copy-done.3, ...), custom_call_target="tpu_custom_call" | custom-call | tf_op jit(solution)/shard_map/vocoder/pallas_call | solution.py:372
  42.6 0.7 %copy.19 = f32[4,1,16384]{2,1,0:T(1,128)} copy(f32[4,1,16384]{2,1,0:T(1,128)S(1)} %bitcast.7) | data formatting | bytes 524288
Async XLA Ops:
  1.8 2.2 %copy-start = (bf16[16,512,256]{2,1,0:T(8,128)(2,1)S(1)}, bf16[16,512,256]{2,1,0:T(8,128)(2,1)}, u32[]{:S(2)}) copy-start(bf16[16,512,256]{2,1,0:T(8,128)(2,1)} %up1_hbm.1) | copy-start | bytes 12582916
  4.0 1.2 %copy-start.1 = (bf16[16,256,128]{2,1,0:T(8,128)(2,1)S(1)}, bf16[16,256,128]{2,1,0:T(8,128)(2,1)}, u32[]{:S(2)}) copy-start(bf16[16,256,128]{2,1,0:T(8,128)(2,1)} %up2_hbm.1) | copy-start | bytes 3145732
  5.2 0.9 %copy-start.2 = (bf16[64,8,256]{2,1,0:T(8,128)(2,1)S(1)}, bf16[64,8,256]{2,1,0:T(8,128)(2,1)}, u32[]{:S(2)}) copy-start(bf16[64,8,256]{2,1,0:T(8,128)(2,1)} %param.14) | copy-start | bytes 786436
  6.2 0.8 %copy-start.3 = (bf16[3,64,64]{2,1,0:T(8,128)(2,1)S(1)}, bf16[3,64,64]{2,1,0:T(8,128)(2,1)}, u32[]{:S(2)}) copy-start(bf16[3,64,64]{2,1,0:T(8,128)(2,1)} %res3_ref.1) | copy-start | bytes 73732
  7.0 0.7 %copy-start.4 = (bf16[3,32,32]{2,1,0:T(8,128)(2,1)S(1)}, bf16[3,32,32]{2,1,0:T(8,128)(2,1)}, u32[]{:S(2)}) copy-start(bf16[3,32,32]{2,1,0:T(8,128)(2,1)} %res4_ref.1) | copy-start | bytes 18436
  7.7 0.7 %copy-start.5 = (bf16[7,32]{1,0:T(8,128)(2,1)S(1)}, bf16[7,32]{1,0:T(8,128)(2,1)}, u32[]{:S(2)}) copy-start(bf16[7,32]{1,0:T(8,128)(2,1)} %post_ref.1) | copy-start | bytes 1348
  8.4 0.7 %copy-start.6 = (s32[512,1]{0,1:T(1,128)S(1)}, s32[512,1]{0,1:T(1,128)}, u32[]{:S(2)}) copy-start(s32[512,1]{0,1:T(1,128)} %param.23) | copy-start | bytes 6148
  9.1 0.7 %copy-start.7 = (s32[512]{0:T(512)S(1)}, s32[512]{0:T(512)}, u32[]{:S(2)}) copy-start(s32[512]{0:T(512)} %param.24) | copy-start | bytes 6148
  9.8 0.7 %copy-start.8 = (s32[512]{0:T(512)S(1)}, s32[512]{0:T(512)}, u32[]{:S(2)}) copy-start(s32[512]{0:T(512)} %param.25) | copy-start | bytes 6148
  10.5 0.7 %copy-start.9 = (s32[512]{0:T(512)S(1)}, s32[512]{0:T(512)}, u32[]{:S(2)}) copy-start(s32[512]{0:T(512)} %param.26) | copy-start | bytes 6148
  11.1 0.7 %copy-start.10 = (s32[512]{0:T(512)S(1)}, s32[512]{0:T(512)}, u32[]{:S(2)}) copy-start(s32[512]{0:T(512)} %param.27) | copy-start | bytes 6148
where the time goes:
time: 43.9 us; the launch traced here: 43.3 us
  Pallas kernels  30.7 us (70%)
  local copies, waits for them, and re-layouts  12.5 us (28%)
    pallas_call x1, Pallas kernels, shards(): pl.pallas_call(functools.partial(kernel, sections, lanes), out_shape=jax....  30.7 us
    unnamed x25, local copies, waits for them, and re-layouts  12.5 us

commit v1 on v0

--- a/solution.py
+++ b/solution.py
@@ -31,6 +31,10 @@
 
 def dot_nt(lhs, rhs):
     return lax.dot_general(lhs, rhs, (((1,), (1,)), ((), ())), preferred_element_type=F32)
+
+
+def dot_tn(lhs, rhs):
+    return lax.dot_general(lhs, rhs, (((0,), (0,)), ((), ())), preferred_element_type=F32)
 
 
 def shifted(values, step, frames):
@@ -54,11 +58,11 @@
         out_ref[place * depth : (place + 1) * depth, :] = block.astype(BF16)
 
 
-def spread_taps(w_ref, copies):
-    taps, _, width = w_ref.shape
+def spread_taps(w_ref, copies, flipped):
+    taps, width = w_ref.shape[0], w_ref.shape[1 if flipped else 2]
     lanes = width * copies
     repeat = ((iota((width, lanes), 1) & (width - 1)) == iota((width, lanes), 0)).astype(F32).astype(BF16)
-    return [dot(w_ref[tap], repeat) for tap in range(taps)]
+    return [(dot_tn if flipped else dot)(w_ref[tap], repeat) for tap in range(taps)]
 
 
 def up_tap(time, out_time):
@@ -162,10 +166,10 @@
         )
         hidden_copies[-1].start()
 
-    assemble(w3_ref, spread_taps(up3_ref, 4), range(-1, 3), range(4), up_tap)
-    assemble(r3_ref, spread_taps(res3_ref, 4), range(-4, 8), range(4), res_tap)
-    assemble(w4_ref, spread_taps(up4_ref, 8), range(-2, 6), range(8), up_tap)
-    assemble(r4_ref, spread_taps(res4_ref, 8), range(-4, 12), range(8), res_tap)
+    assemble(w3_ref, spread_taps(up3_ref, 4, True), range(-1, 3), range(4), up_tap)
+    assemble(r3_ref, spread_taps(res3_ref, 4, False), range(-4, 8), range(4), res_tap)
+    assemble(w4_ref, spread_taps(up4_ref, 8, True), range(-2, 6), range(8), up_tap)
+    assemble(r4_ref, spread_taps(res4_ref, 8, False), range(-4, 12), range(8), res_tap)
     post = post_ref[...].astype(F32)
     channels = post.shape[1]
     span = CHUNK * HOP // PAIRS
@@ -262,7 +266,7 @@
             body(pl.multiple_of(chunk * size, size))
             return carry
 
-        lax.fori_loop(0, PAIRS // CHUNK, step, 0)
+        lax.fori_loop(0, PAIRS // CHUNK, step, 0, unroll=True)
 
     def around(ref, at, whole):
         low = ref[pl.ds(at, size), :]
@@ -367,7 +371,7 @@
     chips = lanes // 2
     total = stream_slot.shape[0]
     vmem = pl.BlockSpec(memory_space=pltpu.VMEM)
-    hbm = pl.BlockSpec(memory_space=pl.ANY)
+    hbm = pl.BlockSpec(memory_space=pltpu.HBM)
     blocks = PAIRS + 2
     out = pl.pallas_call(
         functools.partial(kernel, sections, lanes),
@@ -400,7 +404,7 @@
             pltpu.SemaphoreType.DMA((chips,)),
         ],
         compiler_params=pltpu.CompilerParams(
-            collective_id=0, has_side_effects=True, vmem_limit_bytes=48 * 1024 * 1024
+            collective_id=0, has_side_effects=True, vmem_limit_bytes=63 * 1024 * 1024
         ),
         name="vocoder",
     )(
@@ -408,9 +412,9 @@
         pre_weight,
         up1_weight,
         up2_weight,
-        up3_weight,
+        jnp.swapaxes(up3_weight, 1, 2),
         res3_weight,
-        up4_weight,
+        jnp.swapaxes(up4_weight, 1, 2),
         res4_weight,
         post_weight,
         owner_device.reshape(1, total),

time: 43.9 us -> 29.2 us (0.67)
  the two profiles are of different devices: /device:TPU:5 before, /device:TPU:1 now
where the time goes in v1:
time: 29.2 us; the launch traced here: 28.8 us
  Pallas kernels  27.1 us (93%)
  local copies, waits for them, and re-layouts  1.67 us (6%)
    pallas_call x1, Pallas kernels, shards(): pl.pallas_call(functools.partial(kernel, sections, lanes), out_shape=jax....  27.1 us
    unnamed x1, local copies, waits for them, and re-layouts  1.67 us

profile of v1, /device:TPU:1, one launch (start us, length us, event | category | flops | bytes accessed | tf_op | source)
XLA Modules:
  0.0 28.8 jit_solution(2716733698508704184)
XLA Ops:
  0.0 27.1 %vocoder.1 = f32[512,128]{1,0:T(8,128)} custom-call(bf16[512,256]{1,0:T(8,128)(2,1)} %bitcast.10, bf16[7,1024,512]{2,1,0:T(8,128)(2,1)} %pre_hbm.1, bf16[16,512,256]{2,1,0:T(8,128)(2,1)} %up1_hbm.1, bf16[16,256,128]{2,1,0:T(8,128)(2,1)} %up2_hbm.1, bf16[4,64,128]{2,1,0:T(8,128)(2,1)} %bitcast.11, bf16[3,64,64]{2,1,0:T(8,128)(2,1)} %res3_ref.1, ...), custom_call_target="tpu_custom_call" | custom-call | tf_op jit(solution)/shard_map/vocoder/pallas_call | solution.py:376
  27.1 1.7 %copy.17 = f32[4,1,16384]{2,1,0:T(1,128)} copy(f32[4,1,16384]{2,1,0:T(1,128)} %bitcast.9) | data formatting | bytes 524288

commit v2 on v1

--- a/solution.py
+++ b/solution.py
@@ -11,7 +11,9 @@
 STR_DEV = 4
 SLF = 64
 PAIRS = 32
-CHUNK = 4
+CHUNK = 8
+REACH = 4
+PARTS = 2
 MESH = pl.DeviceIdType.MESH
 F32 = jnp.float32
 BF16 = jnp.bfloat16
@@ -129,11 +131,12 @@
     def block(index):
         return pl.ds(pl.multiple_of(index * rows, rows), rows)
 
+    pre_taps = pre_ref.shape[0]
     copies = [
-        pltpu.make_async_copy(pre_hbm, pre_ref, weight_sem.at[0]),
-        pltpu.make_async_copy(up1_hbm, up1_ref, weight_sem.at[1]),
-        pltpu.make_async_copy(up2_hbm, up2_ref, weight_sem.at[2]),
+        pltpu.make_async_copy(pre_hbm.at[tap], pre_ref.at[tap], weight_sem.at[tap]) for tap in range(pre_taps)
     ]
+    copies.append(pltpu.make_async_copy(up1_hbm, up1_ref, weight_sem.at[pre_taps]))
+    copies.append(pltpu.make_async_copy(up2_hbm, up2_ref, weight_sem.at[pre_taps + 1]))
     own = pltpu.make_async_copy(hidden_ref.at[block(section)], x_ref.at[block(section)], own_sem)
 
     barrier = pltpu.get_barrier_semaphore()
@@ -172,7 +175,7 @@
     assemble(r4_ref, spread_taps(res4_ref, 8, False), range(-4, 12), range(8), res_tap)
     post = post_ref[...].astype(F32)
     channels = post.shape[1]
-    span = CHUNK * HOP // PAIRS
+    span = REACH * HOP // PAIRS
     eye = (iota((channels, channels), 0) == iota((channels, channels), 1)).astype(F32).astype(BF16)
     post_taps = [
         dot_nt(eye, jnp.broadcast_to(post[tap : tap + 1], (128, channels)).astype(BF16)) for tap in range(7)
@@ -197,53 +200,54 @@
     )
     facts = facts.astype(F32).astype(BF16)
     lane_groups = sections * groups
-    per_tile = 128 // lane_groups
     row_group = iota((rows, total), 0) // frames
     mine = (iota((rows, total), 1) == lane * lane_groups + section * groups + row_group).astype(F32).astype(BF16)
     fades = dot_nt(mine, facts)
     lead, tail = fades[:, 2:3], fades[:, 3:4]
-    column_group = iota((128, rows), 1) // frames
-    column_frame = iota((1, rows), 1) & (frames - 1)
-    target_row = iota((STR_DEV * SLF, rows), 0)
-    for sub in range(per_tile):
-        pick = (iota((128, rows), 0) == sub * lane_groups + section * groups + column_group).astype(F32).astype(BF16)
+    part_rows = rows // PARTS
+    column = iota((128, 128), 1)
+    column_frame = iota((1, 128), 1) & (frames - 1)
+    target_row = iota((STR_DEV * SLF, 128), 0)
+    for part in range(PARTS):
+        group = part * (groups // PARTS) + (column & (part_rows - 1)) // frames
+        pick_row = column // part_rows * lane_groups + section * groups + group
+        pick = (iota((128, 128), 0) == pick_row).astype(F32).astype(BF16)
         for tile in range(total // 128):
-            source = tile * per_tile + sub
             found = dot(facts[:, tile * 128 : (tile + 1) * 128], pick)
             owner = found[0:1].astype(jnp.int32)
             target = jnp.where(owner == lane, found[1:2].astype(jnp.int32) + column_frame, -1)
-            place_ref[:, source * rows : (source + 1) * rows] = (
-                (target_row == target).astype(F32).astype(BF16)
-            )
+            at = part * lanes * part_rows + tile * 128
+            place_ref[:, at : at + 128] = (target_row == target).astype(F32).astype(BF16)
 
     own.wait()
-    copies[0].wait()
     for copy in hidden_copies:
         copy.wait()
     x = jnp.concatenate([x_ref[part * rows : (part + 1) * rows, :] for part in range(sections)], axis=1)
-    projected = dot(x, pre_ref[3])
-    for tap in (0, 1, 2, 4, 5, 6):
-        projected = projected + shifted(dot(x, pre_ref[tap]), tap - 3, frames)
+    projected = jnp.zeros((rows, pre_ref.shape[2]), F32)
+    for tap in range(pre_taps):
+        copies[tap].wait()
+        projected = projected + shifted(dot(x, pre_ref[tap]), tap - pre_taps // 2, frames)
     active = leaky(projected, 0.1)
     now = active.astype(BF16)
     before = shifted(active, -1, frames).astype(BF16)
     after = shifted(active, 1, frames).astype(BF16)
 
-    copies[1].wait()
+    copies[pre_taps].wait()
     for phase in range(8):
         other, tap = (before, phase + 12) if phase < 4 else (after, phase - 4)
         up = dot(now, up1_ref[phase + 4]) + dot(other, up1_ref[tap])
         a1_ref[(phase + 1) * rows : (phase + 2) * rows, :] = leaky(up, 0.1).astype(BF16)
 
-    def fill_ends(ref, count):
-        last = ref[count * rows : (count + 1) * rows, :].astype(F32)
-        ref[0:rows, :] = shifted(last, -1, frames).astype(BF16)
-        first = ref[rows : 2 * rows, :].astype(F32)
-        ref[(count + 1) * rows : (count + 2) * rows, :] = shifted(first, 1, frames).astype(BF16)
-
-    fill_ends(a1_ref, 8)
-
-    copies[2].wait()
+    def fill_ends(ref, base, count, depth):
+        def at(index):
+            return slice(base + index * depth, base + (index + 1) * depth)
+
+        ref[at(0), :] = shifted(ref[at(count), :].astype(F32), -1, frames).astype(BF16)
+        ref[at(count + 1), :] = shifted(ref[at(1), :].astype(F32), 1, frames).astype(BF16)
+
+    fill_ends(a1_ref, 0, 8, rows)
+
+    copies[pre_taps + 1].wait()
     for pair in range(4):
         near = 2 * pair + 4
         far, offset = (2 * pair + 12, 0) if pair < 2 else (2 * pair - 4, 2)
@@ -255,95 +259,115 @@
             there = a1_ref[(low + offset) * rows : (low + offset + 4) * rows, :]
             up = leaky(dot(here, near_w) + dot(there, far_w), 0.1).astype(BF16)
             for phase in range(4):
-                to = (low + phase) * 4 + pair + 1
-                a_ref[to * rows : (to + 1) * rows, :] = up[phase * rows : (phase + 1) * rows]
-    fill_ends(a_ref, PAIRS)
-
-    size = CHUNK * rows
-
-    def each_chunk(body):
-        def step(chunk, carry):
-            body(pl.multiple_of(chunk * size, size))
-            return carry
-
-        lax.fori_loop(0, PAIRS // CHUNK, step, 0, unroll=True)
+                for part in range(PARTS):
+                    to = part * (PAIRS + 2) + (low + phase) * 4 + pair + 1
+                    a_ref[to * part_rows : (to + 1) * part_rows, :] = up[
+                        phase * rows + part * part_rows : phase * rows + (part + 1) * part_rows
+                    ]
+
+    size = CHUNK * part_rows
 
     def around(ref, at, whole):
-        low = ref[pl.ds(at, size), :]
-        mid = ref[pl.ds(pl.multiple_of(at + rows, rows), size), :]
-        high = ref[pl.ds(pl.multiple_of(at + 2 * rows, rows), size), :]
+        low = ref[at : at + size, :]
+        mid = ref[at + part_rows : at + part_rows + size, :]
+        high = ref[at + 2 * part_rows : at + 2 * part_rows + size, :]
         if not whole:
             low, high = low[:, 128:], high[:, :128]
         return jnp.concatenate([low, mid, high], axis=1)
 
-    def upsample(w_ref):
-        def body(at):
-            up = dot(around(a_ref, at, False), w_ref[...])
-            u_ref[pl.ds(at, size), :] = up
-            i_ref[pl.ds(pl.multiple_of(at + rows, rows), size), :] = leaky(up, 0.1).astype(BF16)
-
-        each_chunk(body)
-        fill_ends(i_ref, PAIRS)
-
-    def residual(w_ref, whole, slope):
-        def body(at):
-            middle = u_ref[pl.ds(at, size), :] + dot(around(i_ref, at, whole), w_ref[...])
-            a_ref[pl.ds(pl.multiple_of(at + rows, rows), size), :] = leaky(middle, slope).astype(BF16)
-
-        each_chunk(body)
-        fill_ends(a_ref, PAIRS)
-
-    upsample(w3_ref)
-    residual(r3_ref, True, 0.1)
-    upsample(w4_ref)
-    residual(r4_ref, False, 0.01)
-
-    post_w = wp_ref[...]
-    halves = []
-    column = iota((rows, 128), 1) // span
-    for half in range(2):
-        merged = jnp.zeros((rows, 128), F32)
-        for part in range(128 // span):
-            first = (half * (128 // span) + part) * CHUNK
-            pieces = [a_ref[first * rows : (first + 1) * rows, 128:]]
-            pieces += [a_ref[(first + 1 + p) * rows : (first + 2 + p) * rows, :] for p in range(CHUNK)]
-            pieces += [a_ref[(first + 1 + CHUNK) * rows : (first + 2 + CHUNK) * rows, :128]]
-            merged = jnp.where(column == part, dot(jnp.concatenate(pieces, axis=1), post_w), merged)
-        halves.append(merged)
-    wave = jnp.tanh(jnp.concatenate(halves, axis=1))
-    frame = iota((rows, HOP), 0) & (frames - 1)
-    sample = (frame * HOP + iota((rows, HOP), 1)).astype(F32) + 0.5
-    ramp_in = jnp.minimum(1.0, sample / (HOP * lead))
-    ramp_out = jnp.minimum(1.0, (frames * HOP - sample) / (HOP * tail))
-    wave_ref[block(lane), :] = (wave * (ramp_in * ramp_out)).astype(BF16)
-
-    def send(index, peer, send_sem, recv_sem):
-        return pltpu.make_async_remote_copy(
-            src_ref=wave_ref.at[block(index)],
-            dst_ref=wave_ref.at[block(index)],
+    def upsample(base, w_ref):
+        for at in range(0, PAIRS * part_rows, size):
+            up = dot(around(a_ref, base + at, False), w_ref[...])
+            u_ref[at : at + size, :] = up
+            i_ref[at + part_rows : at + part_rows + size, :] = leaky(up, 0.1).astype(BF16)
+        fill_ends(i_ref, 0, PAIRS, part_rows)
+
+    def residual(base, w_ref, whole, slope):
+        for at in range(0, PAIRS * part_rows, size):
+            middle = u_ref[at : at + size, :] + dot(around(i_ref, at, whole), w_ref[...])
+            to = base + part_rows + at
+            a_ref[to : to + size, :] = leaky(middle, slope).astype(BF16)
+        fill_ends(a_ref, base, PAIRS, part_rows)
+
+    def output(base, part):
+        blocks = PAIRS // REACH
+        pieces = []
+        for piece in range(REACH + 2):
+            low, high = (128, 256) if piece == 0 else (0, 128) if piece == REACH + 1 else (0, 256)
+            firsts = [base + (at * REACH + piece) * part_rows for at in range(blocks)]
+            pieces.append(jnp.concatenate([a_ref[at : at + part_rows, low:high] for at in firsts], axis=0))
+        summed = dot(jnp.concatenate(pieces, axis=1), wp_ref[...])
+        column = iota((part_rows, 128), 1) // span
+        halves = []
+        for half in range(HOP // 128):
+            merged = jnp.zeros((part_rows, 128), F32)
+            for place in range(128 // span):
+                first = (half * (128 // span) + place) * part_rows
+                merged = jnp.where(column == place, summed[first : first + part_rows], merged)
+            halves.append(merged)
+        wave = jnp.tanh(jnp.concatenate(halves, axis=1))
+        frame = iota((part_rows, HOP), 0) & (frames - 1)
+        sample = (frame * HOP + iota((part_rows, HOP), 1)).astype(F32) + 0.5
+        here = slice(part * part_rows, (part + 1) * part_rows)
+        ramp_in = jnp.minimum(1.0, sample / (HOP * lead[here]))
+        ramp_out = jnp.minimum(1.0, (frames * HOP - sample) / (HOP * tail[here]))
+        wave_ref[wave_block(part, lane), :] = (wave * (ramp_in * ramp_out)).astype(BF16)
+
+    def wave_block(part, index):
+        return pl.ds(pl.multiple_of((part * lanes + index) * part_rows, part_rows), part_rows)
+
+    def send(part, index, peer, send_sem, recv_sem):
+        copy = pltpu.make_async_remote_copy(
+            src_ref=wave_ref.at[wave_block(part, index)],
+            dst_ref=wave_ref.at[wave_block(part, index)],
             send_sem=send_sem,
             recv_sem=recv_sem,
             device_id={"group": peer},
             device_id_type=MESH,
         )
-
-    direct = []
-    for step in range(1, chips):
-        direct.append(send(lane, ((chip + step) % chips) * 2 + core, wave_send.at[step], wave_recv.at[step]))
-        direct[-1].start()
-    to_sibling = [send(lane, sibling, fwd_send.at[0], fwd_recv.at[0])]
-    to_sibling[0].start()
-    for step in range(1, chips):
-        direct[step - 1].wait_recv()
-        source = ((chip - step + chips) % chips) * 2 + core
-        to_sibling.append(send(source, sibling, fwd_send.at[step], fwd_recv.at[step]))
-        to_sibling[-1].start()
-    for copy in to_sibling:
-        copy.wait_recv()
-    placed = dot(place_ref[...], wave_ref[...])
+        copy.start()
+        return copy
+
+    direct, to_sibling = {}, {}
+
+    def send_wave(part):
+        for step in range(1, chips):
+            peer = ((chip + step) % chips) * 2 + core
+            direct[part, step] = send(part, lane, peer, wave_send.at[part, step], wave_recv.at[part, step])
+        to_sibling[part, 0] = send(part, lane, sibling, fwd_send.at[part, 0], fwd_recv.at[part, 0])
+
+    def pass_on(part):
+        for step in range(1, chips):
+            direct[part, step].wait_recv()
+            source = ((chip - step + chips) % chips) * 2 + core
+            to_sibling[part, step] = send(
+                part, source, sibling, fwd_send.at[part, step], fwd_recv.at[part, step]
+            )
+
+    def place(part):
+        for step in range(chips):
+            to_sibling[part, step].wait_recv()
+        span_rows = slice(part * lanes * part_rows, (part + 1) * lanes * part_rows)
+        return dot(place_ref[:, span_rows], wave_ref[span_rows, :])
+
+    for part in range(PARTS):
+        base = part * (PAIRS + 2) * part_rows
+        fill_ends(a_ref, base, PAIRS, part_rows)
+        upsample(base, w3_ref)
+        residual(base, r3_ref, True, 0.1)
+        upsample(base, w4_ref)
+        residual(base, r4_ref, False, 0.01)
+        if part:
+            pass_on(part - 1)
+        output(base, part)
+        send_wave(part)
+    placed = place(0)
+    pass_on(PARTS - 1)
+    for part in range(1, PARTS):
+        placed = placed + place(part)
     out_ref[pl.ds(0, STR_DEV * SLF, stride=2), :] = placed[:, :128]
     out_ref[pl.ds(1, STR_DEV * SLF, stride=2), :] = placed[:, 128:]
-    for copy in direct + to_sibling:
+    for copy in list(direct.values()) + list(to_sibling.values()):
         copy.wait_send()
 
 
@@ -375,7 +399,7 @@
     blocks = PAIRS + 2
     out = pl.pallas_call(
         functools.partial(kernel, sections, lanes),
-        out_shape=jax.ShapeDtypeStruct((STR_DEV * SLF * HOP // 128, 128), F32),
+        out_shape=pltpu.VMEM((STR_DEV * SLF * HOP // 128, 128), F32),
         in_specs=[hbm] * 4 + [vmem] * 10,
         out_specs=vmem,
         scratch_shapes=[
@@ -385,23 +409,23 @@
             pltpu.VMEM(up2_weight.shape, BF16),
             pltpu.VMEM((10 * rows, 256), BF16),
             pltpu.VMEM((blocks * rows, 256), BF16),
-            pltpu.VMEM((blocks * rows, 256), BF16),
-            pltpu.VMEM((PAIRS * rows, 256), F32),
+            pltpu.VMEM((blocks * rows // PARTS, 256), BF16),
+            pltpu.VMEM((PAIRS * rows // PARTS, 256), F32),
             pltpu.VMEM((512, 256), BF16),
             pltpu.VMEM((768, 256), BF16),
             pltpu.VMEM((512, 256), BF16),
             pltpu.VMEM((512, 256), BF16),
-            pltpu.VMEM(((CHUNK * HOP // PAIRS + 8) * 32, 128), BF16),
+            pltpu.VMEM(((REACH * HOP // PAIRS + 8) * 32, 128), BF16),
             pltpu.VMEM((STR_DEV * SLF, lanes * rows), BF16),
             pltpu.VMEM((lanes * rows, HOP), BF16),
-            pltpu.SemaphoreType.DMA((3,)),
+            pltpu.SemaphoreType.DMA((pre_weight.shape[0] + 2,)),
             pltpu.SemaphoreType.DMA,
             pltpu.SemaphoreType.DMA((sections,)),
             pltpu.SemaphoreType.DMA((sections,)),
-            pltpu.SemaphoreType.DMA((chips,)),
-            pltpu.SemaphoreType.DMA((chips,)),
-            pltpu.SemaphoreType.DMA((chips,)),
-            pltpu.SemaphoreType.DMA((chips,)),
+            pltpu.SemaphoreType.DMA((PARTS, chips)),
+            pltpu.SemaphoreType.DMA((PARTS, chips)),
+            pltpu.SemaphoreType.DMA((PARTS, chips)),
+            pltpu.SemaphoreType.DMA((PARTS, chips)),
         ],
         compiler_params=pltpu.CompilerParams(
             collective_id=0, has_side_effects=True, vmem_limit_bytes=63 * 1024 * 1024

time: 29.2 us -> 30.7 us (1.051)
  Pallas kernels: 27.1 us -> 29.8 us
  local copies, waits for them, and re-layouts: 1.67 us -> 0.71 us
    pallas_call x1, Pallas kernels: 27.1 us -> 29.8 us  [shards(): pl.pallas_call(functools.partial(kernel, sections, lanes), out_shape=pltp...]
    unnamed x1, local copies, waits for them, and re-layouts: 1.67 us -> 0.71 us
where the time goes in v2:
time: 30.7 us; the launch traced here: 30.5 us
  Pallas kernels  29.8 us (97%)
  local copies, waits for them, and re-layouts  0.71 us (2%)
    pallas_call x1, Pallas kernels, shards(): pl.pallas_call(functools.partial(kernel, sections, lanes), out_shape=pltp...  29.8 us
    unnamed x1, local copies, waits for them, and re-layouts  0.71 us

profile of v2, /device:TPU:1, one launch (start us, length us, event | category | flops | bytes accessed | tf_op | source)
XLA Modules:
  0.0 30.5 jit_solution(16886902511206361110)
XLA Ops:
  0.0 29.8 %vocoder.1 = f32[512,128]{1,0:T(8,128)S(1)} custom-call(bf16[512,256]{1,0:T(8,128)(2,1)} %bitcast.10, bf16[7,1024,512]{2,1,0:T(8,128)(2,1)} %pre_hbm.1, bf16[16,512,256]{2,1,0:T(8,128)(2,1)} %up1_hbm.1, bf16[16,256,128]{2,1,0:T(8,128)(2,1)} %up2_hbm.1, bf16[4,64,128]{2,1,0:T(8,128)(2,1)} %bitcast.11, bf16[3,64,64]{2,1,0:T(8,128)(2,1)} %res3_ref.1, ...), custom_call_target="tpu_custom_call" | custom-call | tf_op jit(solution)/shard_map/vocoder/pallas_call | solution.py:400
  29.8 0.7 %copy.17 = f32[4,1,16384]{2,1,0:T(1,128)} copy(f32[4,1,16384]{2,1,0:T(1,128)S(1)} %bitcast.9) | data formatting | bytes 524288

commit v3 on v2

--- a/solution.py
+++ b/solution.py
@@ -11,7 +11,7 @@
 STR_DEV = 4
 SLF = 64
 PAIRS = 32
-CHUNK = 8
+CHUNK = 4
 REACH = 4
 PARTS = 2
 MESH = pl.DeviceIdType.MESH
@@ -96,6 +96,8 @@
     tail_ref,
     out_ref,
     x_ref,
+    part_ref,
+    others_ref,
     pre_ref,
     up1_ref,
     up2_ref,
@@ -131,13 +133,14 @@
     def block(index):
         return pl.ds(pl.multiple_of(index * rows, rows), rows)
 
-    pre_taps = pre_ref.shape[0]
+    taps, width = pre_ref.shape[0], pre_ref.shape[1]
+    features = pl.ds(pl.multiple_of(section * width, width), width)
+    own = pltpu.make_async_copy(hidden_ref, x_ref, own_sem)
     copies = [
-        pltpu.make_async_copy(pre_hbm.at[tap], pre_ref.at[tap], weight_sem.at[tap]) for tap in range(pre_taps)
+        pltpu.make_async_copy(pre_hbm.at[:, features, :], pre_ref, weight_sem.at[0]),
+        pltpu.make_async_copy(up1_hbm, up1_ref, weight_sem.at[1]),
+        pltpu.make_async_copy(up2_hbm, up2_ref, weight_sem.at[2]),
     ]
-    copies.append(pltpu.make_async_copy(up1_hbm, up1_ref, weight_sem.at[pre_taps]))
-    copies.append(pltpu.make_async_copy(up2_hbm, up2_ref, weight_sem.at[pre_taps + 1]))
-    own = pltpu.make_async_copy(hidden_ref.at[block(section)], x_ref.at[block(section)], own_sem)
 
     barrier = pltpu.get_barrier_semaphore()
     for step in range(1, sections):
@@ -152,22 +155,34 @@
     own.start()
     for copy in copies:
         copy.start()
+
+    own.wait()
+    x = x_ref[...].astype(F32)
+    windows = jnp.concatenate([shifted(x, tap - taps // 2, frames).astype(BF16) for tap in range(taps)], axis=1)
+    copies[0].wait()
+    pre_w = pre_ref[...].reshape(taps * width, pre_ref.shape[2])
+    everyone = sections * rows
+    halves = pre_ref.shape[2] // 256
+    for half in range(halves):
+        partial = dot(windows, pre_w[:, half * 256 : (half + 1) * 256])
+        u_ref[half * everyone : (half + 1) * everyone, :] = partial
+        part_ref[:, half * 256 : (half + 1) * 256] = partial.astype(BF16)
+
     pl.semaphore_wait(barrier, sections + chips - 1)
-
-    hidden_copies = []
+    partial_copies = []
     for step in range(1, sections):
         peer = (section + step) % sections
-        hidden_copies.append(
+        partial_copies.append(
             pltpu.make_async_remote_copy(
-                src_ref=hidden_ref.at[block(peer)],
-                dst_ref=x_ref.at[block(section)],
+                src_ref=part_ref.at[block(peer)],
+                dst_ref=others_ref.at[pl.ds((step - 1) * rows, rows)],
                 send_sem=hid_send.at[step],
                 recv_sem=hid_recv.at[step],
                 device_id={"section": peer},
                 device_id_type=MESH,
             )
         )
-        hidden_copies[-1].start()
+        partial_copies[-1].start()
 
     assemble(w3_ref, spread_taps(up3_ref, 4, True), range(-1, 3), range(4), up_tap)
     assemble(r3_ref, spread_taps(res3_ref, 4, False), range(-4, 8), range(4), res_tap)
@@ -219,35 +234,36 @@
             at = part * lanes * part_rows + tile * 128
             place_ref[:, at : at + 128] = (target_row == target).astype(F32).astype(BF16)
 
-    own.wait()
-    for copy in hidden_copies:
-        copy.wait()
-    x = jnp.concatenate([x_ref[part * rows : (part + 1) * rows, :] for part in range(sections)], axis=1)
-    projected = jnp.zeros((rows, pre_ref.shape[2]), F32)
-    for tap in range(pre_taps):
-        copies[tap].wait()
-        projected = projected + shifted(dot(x, pre_ref[tap]), tap - pre_taps // 2, frames)
+    projected = jnp.concatenate(
+        [u_ref[pl.ds(pl.multiple_of(half * everyone + section * rows, rows), rows), :] for half in range(halves)],
+        axis=1,
+    )
+    for step in range(1, sections):
+        partial_copies[step - 1].wait()
+        projected = projected + others_ref[(step - 1) * rows : step * rows, :].astype(F32)
     active = leaky(projected, 0.1)
     now = active.astype(BF16)
     before = shifted(active, -1, frames).astype(BF16)
     after = shifted(active, 1, frames).astype(BF16)
 
-    copies[pre_taps].wait()
+    copies[1].wait()
     for phase in range(8):
         other, tap = (before, phase + 12) if phase < 4 else (after, phase - 4)
         up = dot(now, up1_ref[phase + 4]) + dot(other, up1_ref[tap])
         a1_ref[(phase + 1) * rows : (phase + 2) * rows, :] = leaky(up, 0.1).astype(BF16)
 
-    def fill_ends(ref, base, count, depth):
-        def at(index):
-            return slice(base + index * depth, base + (index + 1) * depth)
-
-        ref[at(0), :] = shifted(ref[at(count), :].astype(F32), -1, frames).astype(BF16)
-        ref[at(count + 1), :] = shifted(ref[at(1), :].astype(F32), 1, frames).astype(BF16)
-
-    fill_ends(a1_ref, 0, 8, rows)
-
-    copies[pre_taps + 1].wait()
+    def fill_before(ref, count):
+        last = ref[count * rows : (count + 1) * rows, :].astype(F32)
+        ref[0:rows, :] = shifted(last, -1, frames).astype(BF16)
+
+    def fill_after(ref, count):
+        first = ref[rows : 2 * rows, :].astype(F32)
+        ref[(count + 1) * rows : (count + 2) * rows, :] = shifted(first, 1, frames).astype(BF16)
+
+    fill_before(a1_ref, 8)
+    fill_after(a1_ref, 8)
+
+    copies[2].wait()
     for pair in range(4):
         near = 2 * pair + 4
         far, offset = (2 * pair + 12, 0) if pair < 2 else (2 * pair - 4, 2)
@@ -259,43 +275,77 @@
             there = a1_ref[(low + offset) * rows : (low + offset + 4) * rows, :]
             up = leaky(dot(here, near_w) + dot(there, far_w), 0.1).astype(BF16)
             for phase in range(4):
-                for part in range(PARTS):
-                    to = part * (PAIRS + 2) + (low + phase) * 4 + pair + 1
-                    a_ref[to * part_rows : (to + 1) * part_rows, :] = up[
-                        phase * rows + part * part_rows : phase * rows + (part + 1) * part_rows
-                    ]
-
-    size = CHUNK * part_rows
+                to = (low + phase) * 4 + pair + 1
+                a_ref[to * rows : (to + 1) * rows, :] = up[phase * rows : (phase + 1) * rows]
+    fill_before(a_ref, PAIRS)
+    fill_after(a_ref, PAIRS)
+
+    def level(first, ref, body):
+        chunks = PAIRS // CHUNK
+        for turn in range(chunks):
+            chunk = (first + turn) % chunks
+            body(chunk * CHUNK)
+            if chunk == chunks - 1:
+                fill_before(ref, PAIRS)
+            if chunk == 0:
+                fill_after(ref, PAIRS)
 
     def around(ref, at, whole):
-        low = ref[at : at + size, :]
-        mid = ref[at + part_rows : at + part_rows + size, :]
-        high = ref[at + 2 * part_rows : at + 2 * part_rows + size, :]
+        size = CHUNK * rows
+        low, mid, high = (ref[(at + shift) * rows : (at + shift) * rows + size, :] for shift in range(3))
         if not whole:
             low, high = low[:, 128:], high[:, :128]
         return jnp.concatenate([low, mid, high], axis=1)
 
-    def upsample(base, w_ref):
-        for at in range(0, PAIRS * part_rows, size):
-            up = dot(around(a_ref, base + at, False), w_ref[...])
-            u_ref[at : at + size, :] = up
-            i_ref[at + part_rows : at + part_rows + size, :] = leaky(up, 0.1).astype(BF16)
-        fill_ends(i_ref, 0, PAIRS, part_rows)
-
-    def residual(base, w_ref, whole, slope):
-        for at in range(0, PAIRS * part_rows, size):
-            middle = u_ref[at : at + size, :] + dot(around(i_ref, at, whole), w_ref[...])
-            to = base + part_rows + at
-            a_ref[to : to + size, :] = leaky(middle, slope).astype(BF16)
-        fill_ends(a_ref, base, PAIRS, part_rows)
-
-    def output(base, part):
-        blocks = PAIRS // REACH
+    def upsample(first, w_ref):
+        def body(at):
+            up = dot(around(a_ref, at, False), w_ref[...])
+            u_ref[at * rows : (at + CHUNK) * rows, :] = up
+            i_ref[(at + 1) * rows : (at + 1 + CHUNK) * rows, :] = leaky(up, 0.1).astype(BF16)
+
+        level(first, i_ref, body)
+
+    def residual(first, w_ref):
+        def body(at):
+            middle = u_ref[at * rows : (at + CHUNK) * rows, :] + dot(around(i_ref, at, True), w_ref[...])
+            a_ref[(at + 1) * rows : (at + 1 + CHUNK) * rows, :] = leaky(middle, 0.1).astype(BF16)
+
+        level(first, a_ref, body)
+
+    def gathered(ref, blocks, part, low, high):
+        starts = [index * rows + part * part_rows for index in blocks]
+        return jnp.concatenate([ref[at : at + part_rows, low:high] for at in starts], axis=0)
+
+    def last_residual(first, part):
+        count = CHUNK * PARTS
+        chunks = PAIRS // count
+        for turn in range(chunks):
+            at = (first + turn) % chunks * count
+            lhs = jnp.concatenate(
+                [
+                    gathered(i_ref, range(at, at + count), part, 128, 256),
+                    gathered(i_ref, range(at + 1, at + 1 + count), part, 0, 256),
+                    gathered(i_ref, range(at + 2, at + 2 + count), part, 0, 128),
+                ],
+                axis=1,
+            )
+            middle = gathered(u_ref, range(at, at + count), part, 0, 256) + dot(lhs, r4_ref[...])
+            result = leaky(middle, 0.01).astype(BF16)
+            for index in range(count):
+                to = (at + 1 + index) * rows + part * part_rows
+                a_ref[to : to + part_rows, :] = result[index * part_rows : (index + 1) * part_rows]
+        low = part * part_rows
+        last = a_ref[PAIRS * rows + low : PAIRS * rows + low + part_rows, :].astype(F32)
+        a_ref[low : low + part_rows, :] = shifted(last, -1, frames).astype(BF16)
+        start = a_ref[rows + low : rows + low + part_rows, :].astype(F32)
+        end = (PAIRS + 1) * rows + low
+        a_ref[end : end + part_rows, :] = shifted(start, 1, frames).astype(BF16)
+
+    def output(part):
         pieces = []
         for piece in range(REACH + 2):
             low, high = (128, 256) if piece == 0 else (0, 128) if piece == REACH + 1 else (0, 256)
-            firsts = [base + (at * REACH + piece) * part_rows for at in range(blocks)]
-            pieces.append(jnp.concatenate([a_ref[at : at + part_rows, low:high] for at in firsts], axis=0))
+            pieces.append(gathered(a_ref, range(piece, piece + PAIRS, REACH), part, low, high))
         summed = dot(jnp.concatenate(pieces, axis=1), wp_ref[...])
         column = iota((part_rows, 128), 1) // span
         halves = []
@@ -350,17 +400,14 @@
         span_rows = slice(part * lanes * part_rows, (part + 1) * lanes * part_rows)
         return dot(place_ref[:, span_rows], wave_ref[span_rows, :])
 
+    upsample(0, w3_ref)
+    residual(1, r3_ref)
+    upsample(2, w4_ref)
     for part in range(PARTS):
-        base = part * (PAIRS + 2) * part_rows
-        fill_ends(a_ref, base, PAIRS, part_rows)
-        upsample(base, w3_ref)
-        residual(base, r3_ref, True, 0.1)
-        upsample(base, w4_ref)
-        residual(base, r4_ref, False, 0.01)
-        if part:
-            pass_on(part - 1)
-        output(base, part)
+        last_residual(2, part)
+        output(part)
         send_wave(part)
+    pass_on(0)
     placed = place(0)
     pass_on(PARTS - 1)
     for part in range(1, PARTS):
@@ -404,13 +451,15 @@
         out_specs=vmem,
         scratch_shapes=[
             pltpu.VMEM((sections * rows, width), BF16),
-            pltpu.VMEM(pre_weight.shape, BF16),
+            pltpu.VMEM((sections * rows, pre_weight.shape[2]), BF16),
+            pltpu.VMEM(((sections - 1) * rows, pre_weight.shape[2]), BF16),
+            pltpu.VMEM((pre_weight.shape[0], width, pre_weight.shape[2]), BF16),
             pltpu.VMEM(up1_weight.shape, BF16),
             pltpu.VMEM(up2_weight.shape, BF16),
             pltpu.VMEM((10 * rows, 256), BF16),
             pltpu.VMEM((blocks * rows, 256), BF16),
-            pltpu.VMEM((blocks * rows // PARTS, 256), BF16),
-            pltpu.VMEM((PAIRS * rows // PARTS, 256), F32),
+            pltpu.VMEM((blocks * rows, 256), BF16),
+            pltpu.VMEM((PAIRS * rows, 256), F32),
             pltpu.VMEM((512, 256), BF16),
             pltpu.VMEM((768, 256), BF16),
             pltpu.VMEM((512, 256), BF16),
@@ -418,7 +467,7 @@
             pltpu.VMEM(((REACH * HOP // PAIRS + 8) * 32, 128), BF16),
             pltpu.VMEM((STR_DEV * SLF, lanes * rows), BF16),
             pltpu.VMEM((lanes * rows, HOP), BF16),
-            pltpu.SemaphoreType.DMA((pre_weight.shape[0] + 2,)),
+            pltpu.SemaphoreType.DMA((3,)),
             pltpu.SemaphoreType.DMA,
             pltpu.SemaphoreType.DMA((sections,)),
             pltpu.SemaphoreType.DMA((sections,)),

time: 30.7 us -> 33 us (1.075)
  Pallas kernels: 29.8 us -> 32.2 us
    pallas_call x1, Pallas kernels: 29.8 us -> 32.2 us  [shards(): pl.pallas_call(functools.partial(kernel, sections, lanes), out_shape=pltp...]
where the time goes in v3:
time: 33 us; the launch traced here: 32.9 us
  Pallas kernels  32.2 us (98%)
  local copies, waits for them, and re-layouts  0.71 us (2%)
    pallas_call x1, Pallas kernels, shards(): pl.pallas_call(functools.partial(kernel, sections, lanes), out_shape=pltp...  32.2 us
    unnamed x1, local copies, waits for them, and re-layouts  0.71 us

profile of v3, /device:TPU:1, one launch (start us, length us, event | category | flops | bytes accessed | tf_op | source)
XLA Modules:
  0.0 32.9 jit_solution(12872257375112515035)
XLA Ops:
  0.0 32.2 %vocoder.1 = f32[512,128]{1,0:T(8,128)S(1)} custom-call(bf16[512,256]{1,0:T(8,128)(2,1)} %bitcast.10, bf16[7,1024,512]{2,1,0:T(8,128)(2,1)} %pre_hbm.1, bf16[16,512,256]{2,1,0:T(8,128)(2,1)} %up1_hbm.1, bf16[16,256,128]{2,1,0:T(8,128)(2,1)} %up2_hbm.1, bf16[4,64,128]{2,1,0:T(8,128)(2,1)} %bitcast.11, bf16[3,64,64]{2,1,0:T(8,128)(2,1)} %res3_ref.1, ...), custom_call_target="tpu_custom_call" | custom-call | tf_op jit(solution)/shard_map/vocoder/pallas_call | solution.py:447
  32.2 0.7 %copy.17 = f32[4,1,16384]{2,1,0:T(1,128)} copy(f32[4,1,16384]{2,1,0:T(1,128)S(1)} %bitcast.9) | data formatting | bytes 524288
